TPU v7x, 32 devices: a whole 2x2x4 slice. The times are simulated.
32 devices in a mesh: seq: 8 (over z, x), mp: 2 (over y), role: 2 (over core).
Axes of the slice: x: 2, y: 2, z: 4, core: 2. Of those that a mesh axis runs over, the one named last changes fastest.
Arguments:
- gen_hidden: bfloat16 [8, 16, 3072], P('seq', None, ('mp', 'role')), may hold values from -6 to 6
- gen_out_weight: bfloat16 [3072, 128], P(('mp', 'role')), may hold values from -0.109375 to 0.109375
- patch_order: int32 [8], replicated, may hold values from 0 to 7, each once
- frame_block: int32 [16], replicated, may hold values from 0 to 8, as said below
- embed_weight: bfloat16 [128, 3072], replicated, may hold values from -0.5 to 0.5
- pos_table: bfloat16 [8, 3072], replicated, may hold values from -3 to 3
- norm_gain: bfloat16 [3072], replicated, may hold values from 0.099609375 to 1.8984375
- qkv_weight: bfloat16 [3072, 3, 2048], P(None, None, ('mp', 'role')), may hold values from -0.109375 to 0.109375
- out_weight: bfloat16 [2048, 3072], P(('mp', 'role')), may hold values from -0.125 to 0.125
Outputs:
- disc_out: bfloat16 [128, 3072], P(('seq', 'mp', 'role'))
Inputs may be any that keep to these rules, and one draw needn't show every extreme that they name: `patch_order`: each patch position appears in exactly one slot. `frame_block`: blocks are runs of consecutive frames with indices never falling, each of 1 to 4 frames, at least one of exactly 4; frames share a block iff their indices are equal.
All inputs are finite; a program needn't handle non-finite values.
Results may differ from a plain program's by a relative error of at most 0.006.
Values may be sent and summed in bfloat16 or wider, within the bound.
No kernel may reach another device: no remote copies, remote signals or barrier semaphores. Data moves between devices by JAX's collectives and lax.ppermute only.
A program may use at most 64 MiB of HBM per device.

v0:
```python
import jax
import jax.numpy as jnp
from jax import lax
from jax.sharding import PartitionSpec as P

HS = 128
MOSTB = 4


def from_behind(block, axis, distance):
    devices = range(lax.axis_size(axis))
    route = [(i - distance, i) for i in devices if i - distance in devices]
    return lax.ppermute(block, axis, route)


def prepare(latents, embed_weight, pos_table, norm_gain, qkv_weight):
    frames, patches, channels = latents.shape
    flat = latents.reshape(frames * patches, channels)
    embedded = jnp.dot(flat, embed_weight, preferred_element_type=jnp.float32).reshape(
        frames, patches, -1
    )
    embedded = embedded + pos_table.astype(jnp.float32)[None]
    scale = lax.rsqrt(jnp.mean(embedded * embedded, axis=-1, keepdims=True) + 1e-06)
    normed = (embedded * scale * norm_gain.astype(jnp.float32)).astype(jnp.bfloat16)
    proj = jnp.einsum("fpd,dcm->cfpm", normed, qkv_weight, preferred_element_type=jnp.float32)
    return (embedded, proj.astype(jnp.bfloat16))


def lookup_blocks(frame_ids, frame_block):
    table = jnp.arange(frame_block.shape[0], dtype=jnp.int32)
    hit = frame_ids[:, None] == table[None, :]
    found = jnp.sum(jnp.where(hit, frame_block[None, :], 0), axis=1)
    return jnp.where(jnp.any(hit, axis=1), found, -1)


def on_device(
    gen_hidden,
    gen_out_weight,
    patch_order,
    frame_block,
    embed_weight,
    pos_table,
    norm_gain,
    qkv_weight,
    out_weight,
):
    partial_latents = jnp.einsum(
        "sfd,dc->sfc", gen_hidden, gen_out_weight, preferred_element_type=jnp.float32
    )
    summed = lax.psum(partial_latents, ("mp", "role")).astype(jnp.bfloat16)
    moved = lax.all_to_all(summed, "seq", split_axis=1, concat_axis=0, tiled=True)
    patches = moved.shape[0]
    frame_dev = moved.shape[1]
    inverse = (
        jnp.zeros((patches,), jnp.int32).at[patch_order].set(jnp.arange(patches, dtype=jnp.int32))
    )
    own_latents = jnp.transpose(moved[inverse], (1, 0, 2))
    reach = (MOSTB - 2) // frame_dev + 1
    head_cols = qkv_weight.shape[2]
    embedded, proj = prepare(own_latents, embed_weight, pos_table, norm_gain, qkv_weight)
    query = proj[0]
    own_kv = proj[1:]
    pieces = []
    for offset in range(-reach, reach + 1):
        if offset == 0:
            pieces.append(own_kv)
        else:
            pieces.append(from_behind(own_kv, "seq", -offset))
    window_kv = jnp.concatenate(pieces, axis=1)
    heads_here = head_cols // HS
    rows = frame_dev * patches
    key_frames = window_kv.shape[1]
    device = lax.axis_index("seq")
    query_ids = device * frame_dev + jnp.arange(frame_dev, dtype=jnp.int32)
    key_ids = (device - reach) * frame_dev + jnp.arange(key_frames, dtype=jnp.int32)
    query_blocks = lookup_blocks(query_ids, frame_block)
    key_blocks = lookup_blocks(key_ids, frame_block)
    frame_mask = query_blocks[:, None] == key_blocks[None, :]
    mask = jnp.repeat(jnp.repeat(frame_mask, patches, axis=0), patches, axis=1)
    query_rows = query.reshape(rows, heads_here, HS)
    key_rows = window_kv[0].reshape(key_frames * patches, heads_here, HS)
    value_rows = window_kv[1].reshape(key_frames * patches, heads_here, HS)
    scores = jnp.einsum(
        "qhe,khe->hqk", query_rows, key_rows, preferred_element_type=jnp.float32
    ) / jnp.sqrt(jnp.float32(HS))
    scores = jnp.where(mask[None], scores, jnp.float32(-1e30))
    top = jnp.max(scores, axis=-1, keepdims=True)
    expo = jnp.where(mask[None], jnp.exp(scores - top), jnp.float32(0.0))
    probs = (expo / jnp.sum(expo, axis=-1, keepdims=True)).astype(jnp.bfloat16)
    attn = jnp.einsum("hqk,khe->qhe", probs, value_rows, preferred_element_type=jnp.float32)
    attn = attn.astype(jnp.bfloat16).reshape(rows, head_cols)
    group = lax.axis_size(("mp", "role"))
    share_rows = rows // group
    mixed = lax.psum_scatter(
        jnp.dot(attn, out_weight, preferred_element_type=jnp.float32),
        ("mp", "role"),
        scatter_dimension=0,
        tiled=True,
    )
    flat_embedded = embedded.reshape(rows, -1)
    mine = lax.dynamic_slice_in_dim(
        flat_embedded, lax.axis_index(("mp", "role")) * share_rows, share_rows, 0
    )
    return (mine + mixed).astype(jnp.bfloat16)


def solution(mesh):
    in_specs = (
        P("seq", None, ("mp", "role")),
        P(("mp", "role"), None),
        P(),
        P(),
        P(),
        P(),
        P(),
        P(None, None, ("mp", "role")),
        P(("mp", "role"), None),
    )
    out_specs = P(("seq", "mp", "role"), None)
    return jax.shard_map(
        on_device, mesh=mesh, in_specs=in_specs, out_specs=out_specs, check_vma=False
    )
```

profile of v0, /device:TPU:0, one launch (start us, length us, event | category | flops | bytes accessed | tf_op | source)
XLA Modules:
  0.0 93.8 jit_solution(16541653058816524079)
XLA Ops:
  6.5 0.0 copy-start
  6.5 1.2 %convolution_bitcast_fusion = f32[1,16,128]{2,1,0:T(8,128)S(1)} fusion(bf16[768,128]{1,0:T(8,128)(2,1)} %param.10, bf16[1,16,768]{2,1,0:T(8,128)(2,1)} %param.9), kind=kOutput, calls=%fused_computation.15 | convolution fusion | flops 3145728 | bytes 229376 | tf_op jit(solution)/shard_map/sfd,dc->sfc/dot_general | solution.py:47
  7.8 8.5 %psum.7 = bf16[1,16,128]{2,1,0:T(8,128)(2,1)S(1)} all-reduce(f32[1,16,128]{2,1,0:T(8,128)S(1)} %convolution_bitcast_fusion), channel_id=1, replica_groups=mesh['seq'=8,'mp'=2,'role'=2] {'mp','role'}, use_global_device_ids=true, to_apply=%region_0.0 | all-reduce | flops 2048 | bytes 12288 | tf_op jit(solution)/shard_map/psum | solution.py:50
  16.3 0.6 copy.73
  16.9 5.8 %all-to-all-start = ((bf16[8,2,128]{2,1,0:T(2,128)(2,1)}), bf16[8,2,128]{2,1,0:T(2,128)(2,1)S(1)}, u32[]{:S(2)}, u32[]{:S(2)}) async-start(bf16[8,2,128]{2,1,0:T(2,128)(2,1)} %bitcast.56), calls=%async_computation | async-start | bytes 8192 | tf_op jit(solution)/shard_map/all_to_all | solution.py:51
  22.7 0.0 all-reduce.3.cloned.1.call-start
  22.8 0.2 fusion.28
  22.9 0.8 select_reduce_fusion
  23.8 0.2 fusion.30
  24.0 0.8 select_reduce_fusion.1
  24.8 0.7 compare_select_fusion.1
  25.5 0.6 scatter_custom_fusion
  26.1 0.1 broadcast_compare_fusion
  26.2 0.8 convert_element_type.31
  27.0 0.7 convert_element_type.32
  27.7 0.1 copy.44
  27.8 1.3 %all-to-all-done = bf16[8,2,128]{2,1,0:T(2,128)(2,1)S(1)} async-done(((bf16[8,2,128]{2,1,0:T(2,128)(2,1)}), bf16[8,2,128]{2,1,0:T(2,128)(2,1)S(1)}, u32[]{:S(2)}, u32[]{:S(2)}) %all-to-all-start) | async-done | bytes 4128 | tf_op jit(solution)/shard_map/all_to_all | solution.py:51
  29.1 0.6 gather_fusion
  29.7 1.4 %multiply_reduce_fusion = (f32[2,8]{1,0:T(2,128)S(1)}, f32[2,8,3072]{2,1,0:T(8,128)S(1)}) fusion(f32[8,3072]{1,0:T(8,128)S(1)} %convert_element_type.31, bf16[128,3072]{1,0:T(8,128)(2,1)} %param.13, bf16[2,8,128]{2,0,1:T(2,128)(2,1)S(1)} %bitcast.60), kind=kOutput, calls=%fused_computation.18 | convolution fusion | flops 12730352 | bytes 1085504 | tf_op jit(solution)/shard_map/dot_general | solution.py:19
  31.1 5.1 %fusion.6 = bf16[3,2,8,512]{3,2,0,1:T(8,128)(2,1)S(1)} fusion(bf16[3072,3,512]{2,0,1:T(8,128)(2,1)} %param.16, f32[2,8,3072]{2,1,0:T(8,128)S(1)} %get-tuple-element.8, f32[3072]{0:T(1024)S(1)} %convert_element_type.32, f32[2,8]{1,0:T(2,128)S(1)} %add_rsqrt_fusion), kind=kOutput, calls=%fused_computation.7 | convolution fusion | flops 151166976 | bytes 9695296 | tf_op jit(solution)/shard_map/fpd,dcm->cfpm/dot_general | solution.py:25
  36.2 2.6 %collective-permute-start = (bf16[2,2,8,512]{3,2,0,1:T(8,128)(2,1)S(1)}, bf16[2,2,8,512]{3,2,0,1:T(8,128)(2,1)S(1)}, u32[]{:S(2)}, u32[]{:S(2)}) collective-permute-start(bf16[2,2,8,512]{3,2,0,1:T(8,128)(2,1)S(1)} %slice.19), channel_id=1, source_target_pairs={{0,8},{4,12},{8,16},{12,20},{16,24},{20,28},{1,9},{5,13},{9,17},{1... | collective-permute-start | bytes 98312 | tf_op jit(solution)/shard_map/ppermute | solution.py:13
  38.8 0.7 copy.45
  39.5 4.0 %collective-permute-start.1 = (bf16[2,2,8,512]{3,2,0,1:T(8,128)(2,1)S(1)}, bf16[2,2,8,512]{3,2,0,1:T(8,128)(2,1)}, u32[]{:S(2)}, u32[]{:S(2)}) collective-permute-start(bf16[2,2,8,512]{3,2,0,1:T(8,128)(2,1)S(1)} %slice.19), channel_id=1, source_target_pairs={{0,4},{4,8},{8,12},{12,16},{16,20},{20,24},{24,28},{1,5},{5,9},{9,... | collective-permute-start | bytes 98312 | tf_op jit(solution)/shard_map/ppermute | solution.py:13
  43.4 1.3 %collective-permute-start.2 = (bf16[2,2,8,512]{3,2,0,1:T(8,128)(2,1)S(1)}, bf16[2,2,8,512]{3,2,0,1:T(8,128)(2,1)S(1)}, u32[]{:S(2)}, u32[]{:S(2)}) collective-permute-start(bf16[2,2,8,512]{3,2,0,1:T(8,128)(2,1)S(1)} %slice.19), channel_id=1, source_target_pairs={{4,0},{8,4},{12,8},{16,12},{20,16},{24,20},{28,24},{5,1},{9,5},{13... | collective-permute-start | bytes 98312 | tf_op jit(solution)/shard_map/ppermute | solution.py:13
  44.7 1.3 %collective-permute-start.3 = (bf16[2,2,8,512]{3,2,0,1:T(8,128)(2,1)S(1)}, bf16[2,2,8,512]{3,2,0,1:T(8,128)(2,1)S(1)}, u32[]{:S(2)}, u32[]{:S(2)}) collective-permute-start(bf16[2,2,8,512]{3,2,0,1:T(8,128)(2,1)S(1)} %slice.19), channel_id=1, source_target_pairs={{8,0},{12,4},{16,8},{20,12},{24,16},{28,20},{9,1},{13,5},{17,9},{2... | collective-permute-start | bytes 98312 | tf_op jit(solution)/shard_map/ppermute | solution.py:13
  46.1 0.0 collective-permute-done
  46.1 0.0 collective-permute-done.1
  46.1 0.8 constant_dynamic-update-slice_fusion.3
  46.9 2.4 %collective-permute-done.2 = bf16[2,2,8,512]{3,2,0,1:T(8,128)(2,1)S(1)} collective-permute-done((bf16[2,2,8,512]{3,2,0,1:T(8,128)(2,1)S(1)}, bf16[2,2,8,512]{3,2,0,1:T(8,128)(2,1)S(1)}, u32[]{:S(2)}, u32[]{:S(2)}) %collective-permute-start.2) | collective-permute-done | bytes 32800 | tf_op jit(solution)/shard_map/ppermute | solution.py:13
  49.2 2.2 %collective-permute-done.3 = bf16[2,2,8,512]{3,2,0,1:T(8,128)(2,1)S(1)} collective-permute-done((bf16[2,2,8,512]{3,2,0,1:T(8,128)(2,1)S(1)}, bf16[2,2,8,512]{3,2,0,1:T(8,128)(2,1)S(1)}, u32[]{:S(2)}, u32[]{:S(2)}) %collective-permute-start.3) | collective-permute-done | bytes 32800 | tf_op jit(solution)/shard_map/ppermute | solution.py:13
  51.5 0.6 reshape_squeeze.11
  52.2 1.2 %fusion.34 = (f32[4,16]{1,0:T(4,128)S(1)}, f32[4,16,80]{2,1,0:T(8,128)S(1)}) fusion(pred[16,80]{1,0:T(8,128)(4,1)} %copy.45, bf16[80,4,128]{2,1,0:T(4,128)(2,1)} %reshape_squeeze.11, bf16[16,4,128]{2,1,0:T(4,128)(2,1)S(1)} %reshape_squeeze.10), kind=kOutput, calls=%fused_computation.59 | convolution fusion | flops 1336399 | bytes 120320 | tf_op jit(solution)/shard_map/sub | solution.py:88
  53.4 0.2 fusion.13
  53.6 0.0 copy-done
  53.6 1.2 %fusion.23 = f32[16,3072]{1,0:T(8,128)} fusion(bf16[512,3072]{1,0:T(8,128)(2,1)S(1)} %copy-done, bf16[4,2,8,128]{3,2,1,0:T(8,128)(2,1)S(1)} %fusion.13), kind=kOutput, calls=%fused_computation.29 | convolution fusion | flops 50331648 | bytes 3358720 | tf_op jit(solution)/shard_map/dot_general | solution.py:95
  54.8 0.0 all-reduce.3.cloned.1.call-update
  54.9 1.2 %dynamic-slice = u32[1]{0:T(128)} dynamic-slice(u32[32]{0:T(128)} %constant.46, u32[]{:T(128)S(6)} %add.69), dynamic_slice_sizes={1} | dynamic-slice | bytes 12
  56.8 28.6 %all-reduce.3.cloned.1.call-done = f32[16,3072]{1,0:T(8,128)} async-done(((f32[16,3072]{1,0:T(8,128)}), f32[16,3072]{1,0:T(8,128)}) %all-reduce.3.cloned.1.call-update) | async-done | bytes 196624
  85.4 1.5 %fusion.21 = bf16[4,3072]{1,0:T(4,128)(2,1)} fusion(f32[16,3072]{1,0:T(8,128)} %all-reduce.3.cloned.1.call-done, u32[]{:T(128)S(6)} %multiply.8, f32[16,3072]{1,0:T(8,128)S(1)} %bitcast.57, s32[]{:T(128)S(6)} %select_n.42), kind=kLoop, calls=%fused_computation.25 | loop fusion | flops 24576 | bytes 122888 | tf_op jit(solution)/shard_map/convert_element_type | solution.py:104
  (22 shorter events, 0.2 us)
Async XLA Ops:
  6.5 47.1 %copy-start = (bf16[512,3072]{1,0:T(8,128)(2,1)S(1)}, bf16[512,3072]{1,0:T(8,128)(2,1)}, u32[]{:S(2)}) copy-start(bf16[512,3072]{1,0:T(8,128)(2,1)} %param.17) | copy-start | bytes 9437188
  16.9 12.2 %all-to-all-start = ((bf16[8,2,128]{2,1,0:T(2,128)(2,1)}), bf16[8,2,128]{2,1,0:T(2,128)(2,1)S(1)}, u32[]{:S(2)}, u32[]{:S(2)}) async-start(bf16[8,2,128]{2,1,0:T(2,128)(2,1)} %bitcast.56), calls=%async_computation | async-start | bytes 8192 | tf_op jit(solution)/shard_map/all_to_all | solution.py:51
  22.7 62.7 %all-reduce.3.cloned.1.call-start = ((), (), s32[]{:S(2)}) async-start(), calls=%async_computation.1 | async-start | bytes 393216
  36.2 9.9 %collective-permute-start = (bf16[2,2,8,512]{3,2,0,1:T(8,128)(2,1)S(1)}, bf16[2,2,8,512]{3,2,0,1:T(8,128)(2,1)S(1)}, u32[]{:S(2)}, u32[]{:S(2)}) collective-permute-start(bf16[2,2,8,512]{3,2,0,1:T(8,128)(2,1)S(1)} %slice.19), channel_id=1, source_target_pairs={{0,8},{4,12},{8,16},{12,20},{16,24},{20,28},{1,9},{5,13},{9,17},{1... | collective-permute-start | bytes 98312 | tf_op jit(solution)/shard_map/ppermute | solution.py:13
  39.5 6.6 %collective-permute-start.1 = (bf16[2,2,8,512]{3,2,0,1:T(8,128)(2,1)S(1)}, bf16[2,2,8,512]{3,2,0,1:T(8,128)(2,1)}, u32[]{:S(2)}, u32[]{:S(2)}) collective-permute-start(bf16[2,2,8,512]{3,2,0,1:T(8,128)(2,1)S(1)} %slice.19), channel_id=1, source_target_pairs={{0,4},{4,8},{8,12},{12,16},{16,20},{20,24},{24,28},{1,5},{5,9},{9,... | collective-permute-start | bytes 98312 | tf_op jit(solution)/shard_map/ppermute | solution.py:13
  43.4 5.8 %collective-permute-start.2 = (bf16[2,2,8,512]{3,2,0,1:T(8,128)(2,1)S(1)}, bf16[2,2,8,512]{3,2,0,1:T(8,128)(2,1)S(1)}, u32[]{:S(2)}, u32[]{:S(2)}) collective-permute-start(bf16[2,2,8,512]{3,2,0,1:T(8,128)(2,1)S(1)} %slice.19), channel_id=1, source_target_pairs={{4,0},{8,4},{12,8},{16,12},{20,16},{24,20},{28,24},{5,1},{9,5},{13... | collective-permute-start | bytes 98312 | tf_op jit(solution)/shard_map/ppermute | solution.py:13
  44.7 6.8 %collective-permute-start.3 = (bf16[2,2,8,512]{3,2,0,1:T(8,128)(2,1)S(1)}, bf16[2,2,8,512]{3,2,0,1:T(8,128)(2,1)S(1)}, u32[]{:S(2)}, u32[]{:S(2)}) collective-permute-start(bf16[2,2,8,512]{3,2,0,1:T(8,128)(2,1)S(1)} %slice.19), channel_id=1, source_target_pairs={{8,0},{12,4},{16,8},{20,12},{24,16},{28,20},{9,1},{13,5},{17,9},{2... | collective-permute-start | bytes 98312 | tf_op jit(solution)/shard_map/ppermute | solution.py:13
Sparse Core Ops, SparseCore 0:
  55.0 30.3 all-reduce.2
where the time goes:
time: 94.3 us; the launch traced here: 93.8 us
  waiting for transfers between devices  34.6 us (37%)
  starting transfers between devices  15 us (16%)
  between operations  14.2 us (15%)
  matrix products  10.4 us (11%)
  blocking collectives  8.51 us (9%)
  other arithmetic  5.84 us (6%)
  local copies, waits for them, and re-layouts  5.29 us (6%)
    unnamed x2, waiting for transfers between devices  28.6 us
    ppermute x4, starting transfers between devices, from_behind(): return lax.ppermute(block, axis, route)  9.13 us
    psum x1, blocking collectives, on_device(): summed = lax.psum(partial_latents, ('mp', 'role')).astype(jnp.bfloat16)  8.51 us
    all_to_all x1, starting transfers between devices, on_device(): lax.all_to_all(summed, 'seq', split_axis=1, concat_axis=0, tiled=True)  5.81 us
    dot_general x1, matrix products, prepare(): jnp.einsum('fpd,dcm->cfpm', normed, qkv_weight, preferred_element_type=jn...  5.06 us
    ppermute x4, waiting for transfers between devices, from_behind(): return lax.ppermute(block, axis, route)  4.64 us
    unnamed x10, local copies, waits for them, and re-layouts  2.63 us
  transfers between devices with their start and end apart: 6, of which 4 were waited for; matrix products, arithmetic and copies ran while one was open for 8% of the time, Pallas kernels for 0%

commit v1 on v0

v1 whole, which is shorter than its diff:
```python
import functools

import jax
import jax.numpy as jnp
from jax import lax
from jax.experimental import pallas as pl
from jax.experimental.pallas import tpu as pltpu
from jax.sharding import PartitionSpec as P

HS = 128
MOSTB = 4
REACH = MOSTB - 1
GROUP = ("mp", "role")
EVERY = ("seq", "mp", "role")
CHUNK = 8
VMEM = pl.BlockSpec(memory_space=pltpu.VMEM)
SMEM = pl.BlockSpec(memory_space=pltpu.SMEM)


def dot(a, b):
    return jnp.dot(a, b, preferred_element_type=jnp.float32)


def latent_kernel(frame_dev, hidden_ref, weight_ref, out_ref, padded_ref):
    slots, frames, depth = hidden_ref.shape
    seqs, group, _, window, channels = out_ref.shape
    padded_ref[...] = jnp.zeros_like(padded_ref)
    for slot in range(slots):
        padded_ref[slot, REACH : REACH + frames] = dot(hidden_ref[slot], weight_ref[...])
    for to in range(seqs):
        piece = padded_ref[:, to * frame_dev : to * frame_dev + window]
        for member in range(group):
            out_ref[to, member] = piece


def weights_kernel(embed_ref, pos_ref, gain_ref, weight_ref, scaled_ref, offset_ref):
    channels = embed_ref.shape[0]
    gain = gain_ref[...].astype(jnp.float32)
    left = jnp.concatenate(
        [embed_ref[...].astype(jnp.float32) * gain, pos_ref[...].astype(jnp.float32) * gain], axis=0
    ).astype(jnp.bfloat16)
    both = dot(left, weight_ref[0])
    scaled = both[:channels]
    high = scaled.astype(jnp.bfloat16)
    scaled_ref[0, :channels] = high
    scaled_ref[0, channels:] = (scaled - high.astype(jnp.float32)).astype(jnp.bfloat16)
    offset_ref[0] = both[channels:]


def attend_kernel(
    frame_dev,
    order_ref,
    block_ref,
    partial_ref,
    embed_ref,
    pos_ref,
    scaled_ref,
    offset_ref,
    out_weight_ref,
    mixed_ref,
    mine_ref,
    latent_ref,
    scale_ref,
    own_ref,
):
    seqs, group, slots, window, channels = partial_ref.shape
    patches = seqs * slots
    rows = patches * window
    own_rows = frame_dev * patches
    model = embed_ref.shape[1]
    cols = out_weight_ref.shape[0]
    frames = block_ref.shape[0]
    device = lax.axis_index("seq")
    member = lax.axis_index(GROUP)

    def place(slot):
        total = partial_ref[slot // slots, 0, slot % slots]
        for other in range(1, group):
            total = total + partial_ref[slot // slots, other, slot % slots]
        latent_ref[order_ref[slot]] = total

    if patches <= 16:
        for slot in range(patches):
            place(slot)
    else:
        pl.loop(0, patches)(place)

    chunk = min(CHUNK, patches)

    def measure(step):
        start = step * chunk
        part = latent_ref[pl.ds(start, chunk)].reshape(chunk * window, channels)
        embedded = dot(part.astype(jnp.bfloat16), embed_ref[...]).reshape(chunk, window, model)
        embedded = embedded + pos_ref[pl.ds(start, chunk)].astype(jnp.float32)[:, None]
        mean = jnp.sum(embedded * embedded, axis=-1, keepdims=True) / model
        scale = jnp.broadcast_to(lax.rsqrt(mean + 1e-06), (chunk, window, channels))
        scale_ref[pl.ds(start, chunk)] = scale

    if chunk == patches:
        measure(0)
    else:
        pl.loop(0, patches // chunk)(measure)

    latents = latent_ref[...].reshape(rows, channels).astype(jnp.bfloat16)
    twice = jnp.concatenate([latents, latents], axis=1)
    scale = scale_ref[...].reshape(rows, channels)[:, :1]

    def project(index):
        flat = dot(twice, scaled_ref[index]).reshape(patches, window, cols)
        flat = (flat + offset_ref[index][:, None]).reshape(rows, cols)
        return (flat * scale).astype(jnp.bfloat16)

    key, value = project(1), project(2)

    own = jnp.concatenate(
        [latent_ref[:, REACH + frame, :] for frame in range(frame_dev)], axis=0
    ).astype(jnp.bfloat16)
    pos = pos_ref[...].astype(jnp.float32)
    own_embedded = dot(own, embed_ref[...]) + jnp.concatenate([pos] * frame_dev, axis=0)
    share = own_rows // group
    for other in range(group):
        own_ref[other] = own_embedded[other * share : (other + 1) * share]
    own_mean = jnp.sum(own_embedded * own_embedded, axis=-1, keepdims=True) / model
    own_scale = lax.rsqrt(own_mean + 1e-06)
    query = dot(jnp.concatenate([own, own], axis=1), scaled_ref[0])
    query = (query + jnp.concatenate([offset_ref[0]] * frame_dev, axis=0)) * own_scale
    query = query.astype(jnp.bfloat16)

    def block_of(frame):
        inside = jnp.logical_and(frame >= 0, frame < frames)
        return jnp.where(inside, block_ref[jnp.clip(frame, 0, frames - 1)], -1)

    row_frame = lax.broadcasted_iota(jnp.int32, (own_rows, rows), 0) // patches
    col_frame = lax.broadcasted_iota(jnp.int32, (own_rows, rows), 1) % window
    row_block = jnp.full((own_rows, rows), -2, jnp.int32)
    col_block = jnp.full((own_rows, rows), -1, jnp.int32)
    for frame in range(frame_dev):
        row_block = jnp.where(row_frame == frame, block_of(device * frame_dev + frame), row_block)
    for frame in range(window):
        col_block = jnp.where(
            col_frame == frame, block_of(device * frame_dev - REACH + frame), col_block
        )
    mask = row_block == col_block

    heads = []
    for head in range(cols // HS):
        at = slice(head * HS, (head + 1) * HS)
        scores = lax.dot_general(
            query[:, at], key[:, at], (((1,), (1,)), ((), ())), preferred_element_type=jnp.float32
        ) * (HS**-0.5)
        scores = jnp.where(mask, scores, -1e30)
        top = jnp.max(scores, axis=-1, keepdims=True)
        expo = jnp.where(mask, jnp.exp(scores - top), 0.0)
        probs = (expo / jnp.sum(expo, axis=-1, keepdims=True)).astype(jnp.bfloat16)
        heads.append(dot(probs, value[:, at]).astype(jnp.bfloat16))
    mixed = dot(jnp.concatenate(heads, axis=1), out_weight_ref[...])
    for other in range(group):
        mixed_ref[other] = mixed[other * share : (other + 1) * share].astype(jnp.bfloat16)
    mine_ref[...] = own_ref[member]


def sum_kernel(mine_ref, mixed_ref, out_ref):
    total = mine_ref[...]
    for member in range(mixed_ref.shape[0]):
        total = total + mixed_ref[member].astype(jnp.float32)
    out_ref[...] = total.astype(jnp.bfloat16)


def on_device(
    gen_hidden,
    gen_out_weight,
    patch_order,
    frame_block,
    embed_weight,
    pos_table,
    norm_gain,
    qkv_weight,
    out_weight,
):
    slots, frames, _ = gen_hidden.shape
    channels, model = embed_weight.shape
    cols = qkv_weight.shape[2]
    seqs = lax.axis_size("seq")
    group = lax.axis_size(GROUP)
    patches = seqs * slots
    frame_dev = frames // seqs
    window = frame_dev + 2 * REACH
    own_rows = frame_dev * patches
    share = own_rows // group
    big = pltpu.CompilerParams(vmem_limit_bytes=48 * 1024 * 1024)

    windows = pl.pallas_call(
        functools.partial(latent_kernel, frame_dev),
        out_shape=jax.ShapeDtypeStruct((seqs, group, slots, window, channels), jnp.float32),
        in_specs=[VMEM] * 2,
        out_specs=VMEM,
        scratch_shapes=[pltpu.VMEM((slots, frames + 2 * REACH, channels), jnp.float32)],
        compiler_params=big,
        name="partial_latents",
    )(gen_hidden, gen_out_weight)
    moved = lax.all_to_all(
        windows.reshape(seqs * group, slots, window, channels),
        EVERY,
        split_axis=0,
        concat_axis=0,
        tiled=True,
    ).reshape(seqs, group, slots, window, channels)

    width = cols // 2
    scaled, offset = pl.pallas_call(
        weights_kernel,
        grid=(3, cols // width),
        out_shape=(
            jax.ShapeDtypeStruct((3, 2 * channels, cols), jnp.bfloat16),
            jax.ShapeDtypeStruct((3, patches, cols), jnp.float32),
        ),
        in_specs=[
            pl.BlockSpec((channels, model), lambda i, j: (0, 0)),
            pl.BlockSpec((patches, model), lambda i, j: (0, 0)),
            pl.BlockSpec((1, model), lambda i, j: (0, 0)),
            pl.BlockSpec((1, model, width), lambda i, j: (i, 0, j)),
        ],
        out_specs=(
            pl.BlockSpec((1, 2 * channels, width), lambda i, j: (i, 0, j)),
            pl.BlockSpec((1, patches, width), lambda i, j: (i, 0, j)),
        ),
        compiler_params=pltpu.CompilerParams(vmem_limit_bytes=32 * 1024 * 1024),
        cost_estimate=pl.CostEstimate(
            flops=2 * (channels + patches) * model * 3 * cols,
            bytes_accessed=2 * model * 3 * cols,
            transcendentals=0,
        ),
        name="weight_products",
    )(embed_weight, pos_table, norm_gain.reshape(1, model), jnp.transpose(qkv_weight, (1, 0, 2)))

    mixed, mine = pl.pallas_call(
        functools.partial(attend_kernel, frame_dev),
        out_shape=(
            jax.ShapeDtypeStruct((group, share, model), jnp.bfloat16),
            jax.ShapeDtypeStruct((share, model), jnp.float32),
        ),
        in_specs=[SMEM] * 2 + [VMEM] * 6,
        out_specs=(VMEM, VMEM),
        scratch_shapes=[
            pltpu.VMEM((patches, window, channels), jnp.float32),
            pltpu.VMEM((patches, window, channels), jnp.float32),
            pltpu.VMEM((group, share, model), jnp.float32),
        ],
        compiler_params=big,
        name="attend",
    )(patch_order, frame_block, moved, embed_weight, pos_table, scaled, offset, out_weight)
    mixed = lax.all_to_all(mixed, GROUP, split_axis=0, concat_axis=0, tiled=True)
    return pl.pallas_call(
        sum_kernel,
        out_shape=jax.ShapeDtypeStruct((share, model), jnp.bfloat16),
        in_specs=[VMEM] * 2,
        out_specs=VMEM,
        name="final_sum",
    )(mine, mixed)


def solution(mesh):
    in_specs = (
        P("seq", None, ("mp", "role")),
        P(("mp", "role"), None),
        P(),
        P(),
        P(),
        P(),
        P(),
        P(None, None, ("mp", "role")),
        P(("mp", "role"), None),
    )
    out_specs = P(("seq", "mp", "role"), None)
    return jax.shard_map(
        on_device, mesh=mesh, in_specs=in_specs, out_specs=out_specs, check_vma=False
    )
```

time: 94.3 us -> 34.8 us (0.37)
  waiting for transfers between devices: 34.6 us -> 0.01 us
  between operations: 14.2 us -> 0.07 us
  matrix products: 10.4 us -> 0 us
  Pallas kernels: 0 us -> 8.42 us
  starting transfers between devices: 15 us -> 7.3 us
  local copies, waits for them, and re-layouts: 5.29 us -> 11.2 us
  other arithmetic: 5.84 us -> 0 us
  blocking collectives: 8.51 us -> 7.34 us
    unnamed x2 -> x0, waiting for transfers between devices: 28.6 us -> none
    dot_general x5 -> x0, matrix products: 9.15 us -> none  [the longest x1 5.06 us: prepare(): jnp.einsum('fpd,dcm->cfpm', normed, qkv_weight, preferred_element_type=jn...]
    ppermute x4 -> x0, starting transfers between devices: 9.13 us -> none  [from_behind(): return lax.ppermute(block, axis, route)]
    psum x1 -> x0, blocking collectives: 8.51 us -> none  [on_device(): summed = lax.psum(partial_latents, ('mp', 'role')).astype(jnp.bfloat16)]
    pallas_call x0 -> x4, Pallas kernels: none -> 8.42 us  [the longest x1 3.18 us: on_device(): pl.pallas_call(weights_kernel, grid=(3, cols // width), out_shape=(jax.Sh...]
    unnamed x10 -> x26, local copies, waits for them, and re-layouts: 2.63 us -> 10.4 us
    all_to_all x0 -> x1, blocking collectives: none -> 7.34 us  [on_device(): lax.all_to_all(mixed, GROUP, split_axis=0, concat_axis=0, tiled=True)]
    ppermute x4 -> x0, waiting for transfers between devices: 4.64 us -> none  [from_behind(): return lax.ppermute(block, axis, route)]
  transfers between devices with their start and end apart: 6 -> 1, of which waited for: 4 -> 0; matrix products, arithmetic and copies ran while one was open for 8% -> 2% of each run, Pallas kernels for 0% -> 9%
where the time goes in v1:
time: 34.8 us; the launch traced here: 34.3 us
  local copies, waits for them, and re-layouts  11.2 us (32%)
  Pallas kernels  8.42 us (24%)
  blocking collectives  7.34 us (21%)
  starting transfers between devices  7.3 us (21%)
    unnamed x26, local copies, waits for them, and re-layouts  10.4 us
    all_to_all x1, blocking collectives, on_device(): lax.all_to_all(mixed, GROUP, split_axis=0, concat_axis=0, tiled=True)  7.34 us
    all_to_all x1, starting transfers between devices, on_device(): lax.all_to_all(windows.reshape(seqs * group, slots, window, channels), EV...  7.3 us
    pallas_call x1, Pallas kernels, on_device(): pl.pallas_call(weights_kernel, grid=(3, cols // width), out_shape=(jax.Sh...  3.18 us
    pallas_call x1, Pallas kernels, on_device(): pl.pallas_call(functools.partial(attend_kernel, frame_dev), out_shape=(ja...  2.86 us
    pallas_call x1, Pallas kernels, on_device(): pl.pallas_call(sum_kernel, out_shape=jax.ShapeDtypeStruct((share, model),...  1.55 us
    pallas_call x1, Pallas kernels, on_device(): pl.pallas_call(functools.partial(latent_kernel, frame_dev), out_shape=jax...  0.82 us
    reshape x1, local copies, waits for them, and re-layouts, on_device(): norm_gain.reshape(1, model)  0.7 us
  transfers between devices with their start and end apart: 1, of which 0 were waited for; matrix products, arithmetic and copies ran while one was open for 2% of the time, Pallas kernels for 9%

profile of v1, /device:TPU:0, one launch (start us, length us, event | category | flops | bytes accessed | tf_op | source)
XLA Modules:
  0.0 34.3 jit_solution(7595706076534032061)
XLA Ops:
  0.0 0.0 copy-start.7
  0.0 0.0 copy-start.8
  0.0 0.9 %copy-done.8 = bf16[768,128]{1,0:T(8,128)(2,1)S(1)} copy-done((bf16[768,128]{1,0:T(8,128)(2,1)S(1)}, bf16[768,128]{1,0:T(8,128)(2,1)}, u32[]{:S(2)}) %copy-start.8) | copy-done | bytes 196632
  0.9 0.0 copy-start.10
  0.9 0.7 %copy-done.10 = bf16[1,16,768]{2,1,0:T(8,128)(2,1)S(1)} copy-done((bf16[1,16,768]{2,1,0:T(8,128)(2,1)S(1)}, bf16[1,16,768]{2,1,0:T(8,128)(2,1)}, u32[]{:S(2)}) %copy-start.10) | copy-done | bytes 24600
  1.7 0.0 copy-start.11
  1.7 0.0 copy-start.12
  1.7 0.8 %partial_latents.1 = f32[8,4,1,8,128]{4,3,2,1,0:T(8,128)} custom-call(bf16[1,16,768]{2,1,0:T(8,128)(2,1)S(1)} %copy-done.10, bf16[768,128]{1,0:T(8,128)(2,1)S(1)} %copy-done.8), custom_call_target="tpu_custom_call" | custom-call | tf_op jit(solution)/shard_map/partial_latents/pallas_call | solution.py:192
  2.5 7.3 %all-to-all-start = ((f32[32,1,8,128]{3,2,1,0:T(8,128)}), f32[32,1,8,128]{3,2,1,0:T(8,128)S(1)}, u32[]{:S(2)}, u32[]{:S(2)}) async-start(f32[32,1,8,128]{3,2,1,0:T(8,128)} %bitcast.1), calls=%async_computation | async-start | bytes 262144 | tf_op jit(solution)/shard_map/all_to_all | solution.py:201
  9.8 0.7 %reshape.11.gain_ref = bf16[1,3072]{1,0:T(2,128)(2,1)S(1)} reshape(bf16[3072]{0:T(1024)(128)(2,1)} %param.15) | data formatting | bytes 12288 | tf_op jit(solution)/shard_map/reshape | solution.py:234
  10.5 0.0 copy-start
  10.5 3.7 %copy-done = bf16[3072,3,512]{2,0,1:T(8,128)(2,1)S(1)} copy-done((bf16[3072,3,512]{2,0,1:T(8,128)(2,1)S(1)}, bf16[3072,3,512]{2,0,1:T(8,128)(2,1)}, u32[]{:S(2)}) %copy-start) | copy-done | bytes 9437208
  14.2 0.0 copy-start.2
  14.2 1.1 %copy-done.2 = bf16[128,3072]{1,0:T(8,128)(2,1)S(1)} copy-done((bf16[128,3072]{1,0:T(8,128)(2,1)S(1)}, bf16[128,3072]{1,0:T(8,128)(2,1)}, u32[]{:S(2)}) %copy-start.2) | copy-done | bytes 786456
  15.3 0.0 copy-start.6
  15.3 0.8 %copy-done.6 = bf16[8,3072]{1,0:T(8,128)(2,1)S(1)} copy-done((bf16[8,3072]{1,0:T(8,128)(2,1)S(1)}, bf16[8,3072]{1,0:T(8,128)(2,1)}, u32[]{:S(2)}) %copy-start.6) | copy-done | bytes 49176
  16.1 0.0 copy-start.1
  16.1 3.2 %weight_products.1 = (bf16[3,256,512]{2,1,0:T(8,128)(2,1)S(1)}, f32[3,8,512]{2,1,0:T(8,128)S(1)}) custom-call(bf16[128,3072]{1,0:T(8,128)(2,1)S(1)} %copy-done.2, bf16[8,3072]{1,0:T(8,128)(2,1)S(1)} %copy-done.6, bf16[1,3072]{1,0:T(2,128)(2,1)S(1)} %reshape.11.gain_ref, bf16[3,3072,512]{2,1,0:T(8,128)(2,1)S(1)} %bitcast.5), custom_call_target="tpu_custom_call" | custom-call | flops 1283457024 | bytes 9437184 | tf_op jit(solution)/shard_map/weight_products/pallas_call | solution.py:210
  19.3 0.0 copy-start.4
  19.3 0.9 %copy-done.4 = bf16[3,256,512]{2,1,0:T(8,128)(2,1)} copy-done((bf16[3,256,512]{2,1,0:T(8,128)(2,1)}, bf16[3,256,512]{2,1,0:T(8,128)(2,1)S(1)}, u32[]{:S(2)}) %copy-start.4) | copy-done | bytes 786456
  20.2 0.0 all-to-all-done
  20.2 0.0 copy-done.7
  20.2 0.0 copy-done.11
  20.2 0.0 copy-done.12
  20.2 0.0 copy-done.1
  20.2 0.0 copy-start.3
  20.3 1.1 %copy-done.3 = bf16[128,3072]{1,0:T(8,128)(2,1)S(1)} copy-done((bf16[128,3072]{1,0:T(8,128)(2,1)S(1)}, bf16[128,3072]{1,0:T(8,128)(2,1)}, u32[]{:S(2)}) %copy-start.3) | copy-done | bytes 786456
  21.4 0.0 copy-start.5
  21.4 1.1 %copy-done.5 = bf16[3,256,512]{2,1,0:T(8,128)(2,1)S(1)} copy-done((bf16[3,256,512]{2,1,0:T(8,128)(2,1)S(1)}, bf16[3,256,512]{2,1,0:T(8,128)(2,1)}, u32[]{:S(2)}) %copy-start.5) | copy-done | bytes 786456
  22.5 2.9 %attend.1 = (bf16[4,4,3072]{2,1,0:T(4,128)(2,1)S(1)}, f32[4,3072]{1,0:T(4,128)S(1)}) custom-call(s32[8]{0:T(128)S(1)} %copy-done.11, s32[16]{0:T(128)S(1)} %copy-done.12, f32[8,4,1,8,128]{4,3,2,1,0:T(8,128)S(1)} %bitcast.6, bf16[128,3072]{1,0:T(8,128)(2,1)S(1)} %copy-done.3, bf16[8,3072]{1,0:T(8,128)(2,1)S(1)} %copy-done.7, ...), custom_call_target="tpu_custom_call" | custom-call | tf_op jit(solution)/shard_map/attend/pallas_call | solution.py:236
  25.4 0.0 copy-start.9
  25.4 7.3 %all_to_all.10.mixed_ref = bf16[4,4,3072]{2,1,0:T(4,128)(2,1)} all-to-all(bf16[4,4,3072]{2,1,0:T(4,128)(2,1)S(1)} %get-tuple-element.12), channel_id=1, replica_groups=mesh['seq'=8,'mp'=2,'role'=2] {'mp','role'}, dimensions={0} | all-to-all | bytes 196608 | tf_op jit(solution)/shard_map/all_to_all | solution.py:252
  32.7 0.0 copy-done.9
  32.7 1.6 %final_sum.1 = bf16[4,3072]{1,0:T(4,128)(2,1)} custom-call(f32[4,3072]{1,0:T(4,128)} %copy-done.9, bf16[4,4,3072]{2,1,0:T(4,128)(2,1)} %all_to_all.10.mixed_ref), custom_call_target="tpu_custom_call" | custom-call | tf_op jit(solution)/shard_map/final_sum/pallas_call | solution.py:253
Async XLA Ops:
  0.0 20.2 %copy-start.7 = (bf16[8,3072]{1,0:T(8,128)(2,1)S(1)}, bf16[8,3072]{1,0:T(8,128)(2,1)}, u32[]{:S(2)}) copy-start(bf16[8,3072]{1,0:T(8,128)(2,1)} %pos_ref.3) | copy-start | bytes 147460
  0.0 0.9 %copy-start.8 = (bf16[768,128]{1,0:T(8,128)(2,1)S(1)}, bf16[768,128]{1,0:T(8,128)(2,1)}, u32[]{:S(2)}) copy-start(bf16[768,128]{1,0:T(8,128)(2,1)} %weight_ref.1) | copy-start | bytes 589828
  0.9 0.7 %copy-start.10 = (bf16[1,16,768]{2,1,0:T(8,128)(2,1)S(1)}, bf16[1,16,768]{2,1,0:T(8,128)(2,1)}, u32[]{:S(2)}) copy-start(bf16[1,16,768]{2,1,0:T(8,128)(2,1)} %hidden_ref.1) | copy-start | bytes 73732
  1.7 18.5 %copy-start.11 = (s32[8]{0:T(128)S(1)}, s32[8]{0:T(128)}, u32[]{:S(2)}) copy-start(s32[8]{0:T(128)} %order_ref.1) | copy-start | bytes 100
  1.7 18.6 %copy-start.12 = (s32[16]{0:T(128)S(1)}, s32[16]{0:T(128)}, u32[]{:S(2)}) copy-start(s32[16]{0:T(128)} %block_ref.1) | copy-start | bytes 196
  2.5 17.7 %all-to-all-start = ((f32[32,1,8,128]{3,2,1,0:T(8,128)}), f32[32,1,8,128]{3,2,1,0:T(8,128)S(1)}, u32[]{:S(2)}, u32[]{:S(2)}) async-start(f32[32,1,8,128]{3,2,1,0:T(8,128)} %bitcast.1), calls=%async_computation | async-start | bytes 262144 | tf_op jit(solution)/shard_map/all_to_all | solution.py:201
  10.5 3.7 %copy-start = (bf16[3072,3,512]{2,0,1:T(8,128)(2,1)S(1)}, bf16[3072,3,512]{2,0,1:T(8,128)(2,1)}, u32[]{:S(2)}) copy-start(bf16[3072,3,512]{2,0,1:T(8,128)(2,1)} %param.16) | copy-start | bytes 28311556
  14.2 1.1 %copy-start.2 = (bf16[128,3072]{1,0:T(8,128)(2,1)S(1)}, bf16[128,3072]{1,0:T(8,128)(2,1)}, u32[]{:S(2)}) copy-start(bf16[128,3072]{1,0:T(8,128)(2,1)} %embed_ref.3) | copy-start | bytes 2359300
  15.3 0.8 %copy-start.6 = (bf16[8,3072]{1,0:T(8,128)(2,1)S(1)}, bf16[8,3072]{1,0:T(8,128)(2,1)}, u32[]{:S(2)}) copy-start(bf16[8,3072]{1,0:T(8,128)(2,1)} %pos_ref.3) | copy-start | bytes 147460
  16.1 4.1 %copy-start.1 = (bf16[512,3072]{1,0:T(8,128)(2,1)S(1)}, bf16[512,3072]{1,0:T(8,128)(2,1)}, u32[]{:S(2)}) copy-start(bf16[512,3072]{1,0:T(8,128)(2,1)} %out_weight_ref.1) | copy-start | bytes 9437188
  19.3 0.9 %copy-start.4 = (bf16[3,256,512]{2,1,0:T(8,128)(2,1)}, bf16[3,256,512]{2,1,0:T(8,128)(2,1)S(1)}, u32[]{:S(2)}) copy-start(bf16[3,256,512]{2,1,0:T(8,128)(2,1)S(1)} %get-tuple-element.9.scaled_ref) | copy-start | bytes 2359300
  20.2 1.1 %copy-start.3 = (bf16[128,3072]{1,0:T(8,128)(2,1)S(1)}, bf16[128,3072]{1,0:T(8,128)(2,1)}, u32[]{:S(2)}) copy-start(bf16[128,3072]{1,0:T(8,128)(2,1)} %embed_ref.3) | copy-start | bytes 2359300
  21.4 1.1 %copy-start.5 = (bf16[3,256,512]{2,1,0:T(8,128)(2,1)S(1)}, bf16[3,256,512]{2,1,0:T(8,128)(2,1)}, u32[]{:S(2)}) copy-start(bf16[3,256,512]{2,1,0:T(8,128)(2,1)} %copy-done.4) | copy-start | bytes 2359300
  25.4 7.3 %copy-start.9 = (f32[4,3072]{1,0:T(4,128)}, f32[4,3072]{1,0:T(4,128)S(1)}, u32[]{:S(2)}) copy-start(f32[4,3072]{1,0:T(4,128)S(1)} %get-tuple-element.11.mine_ref) | copy-start | bytes 147460
